TPU v7x, 32 devices: a whole 2x2x4 slice. The times are simulated.
32 devices in a mesh: sec: 2 (over y), gx: 4 (over x, core), gy: 4 (over z).
Axes of the slice: x: 2, y: 2, z: 4, core: 2. Of those that a mesh axis runs over, the one named last changes fastest.
Arguments:
- flow_state: float32 [3, 64, 64, 256], P(None, ('sec', 'gx'), 'gy'), may hold values from -4 to 4
- blade_cells: int32 [3, 64, 128], replicated, may hold values from 0 to 255, as said below
- blade_coef: float32 [64, 128], replicated, may hold values from 0.2 to 2
Outputs:
- flow_next: float32 [3, 64, 64, 256], P(None, ('sec', 'gx'), 'gy')
Inputs may be any that keep to these rules, and one draw needn't show every extreme that they name: `blade_cells`: all 128 points of one turbine share one streamwise index; their spanwise indices lie within 6 cells (periodic over 64) of the turbine's hub and their vertical indices within 6 of the hub's; several points may share a cell; every turbine's hub lies on or one cell below a multiple of 16, and its points lie on both sides of that multiple.
All inputs are finite; a program needn't handle non-finite values.
Results may differ from a plain program's by a relative error of at most 0.00002.
Values sent between devices are 32-bit elements; how exact they have to be, the bound alone decides.
A program may use at most 64 MiB of HBM per device.

v0:
```python
import jax
import jax.numpy as jnp
from jax import lax
from jax.sharding import PartitionSpec as P

time_step = 0.3
viscosity = 0.1
wind_speed = 1.0


def padded_2(x, sides, width):
    for axis, dim in sides:
        peers, length = (lax.axis_size(axis), x.shape[dim])
        up = [(i, (i + 1) % peers) for i in range(peers)]
        down = [(j, i) for i, j in up]
        last = lax.slice_in_dim(x, length - width, length, axis=dim)
        initial = lax.slice_in_dim(x, 0, width, axis=dim)
        before = lax.ppermute(last, axis, up)
        after = lax.ppermute(initial, axis, down)
        x = jnp.concatenate([before, x, after], axis=dim)
    return x


def shifted(x, axis, by):
    peers = lax.axis_size(axis)
    pairs = [(i, i + by) for i in range(peers) if 0 <= i + by < peers]
    return lax.ppermute(x, axis, pairs)


def component_rate(comp, x_plus, x_minus, y_plus, y_minus, vel_x, vel_y, vel_z):
    zero_layer = jnp.zeros_like(comp[:, :, :1])
    z_plus = jnp.concatenate([comp[:, :, 1:], zero_layer], axis=2)
    z_minus = jnp.concatenate([zero_layer, comp[:, :, :-1]], axis=2)
    advection = vel_x * (x_plus - x_minus) + vel_y * (y_plus - y_minus) + vel_z * (z_plus - z_minus)
    laplacian = x_plus + x_minus + y_plus + y_minus + z_plus + z_minus - 6.0 * comp
    return -0.5 * advection + viscosity * laplacian


def body(flow_state, blade_cells, blade_coef):
    n_comp, rows_x, rows_y, rows_z = flow_state.shape
    slab_count = lax.axis_size("gx")
    slab_idx = lax.axis_index("gx")
    span_idx = lax.axis_index("gy")
    sec_idx = lax.axis_index("sec")
    in_farm = sec_idx == 1
    farm_first = jnp.logical_and(in_farm, slab_idx == 0)
    farm_last = jnp.logical_and(in_farm, slab_idx == slab_count - 1)
    cell_x = blade_cells[0].reshape(-1)
    cell_y = blade_cells[1].reshape(-1)
    cell_z = blade_cells[2].reshape(-1)
    owned = jnp.logical_and(
        in_farm, jnp.logical_and(cell_x // rows_x == slab_idx, cell_y // rows_y == span_idx)
    )
    flat_index = (
        (cell_x - slab_idx * rows_x) * rows_y + (cell_y - span_idx * rows_y)
    ) * rows_z + cell_z
    flat_index = jnp.where(owned, flat_index, 0)
    wind_col = jnp.array([wind_speed, 0.0, 0.0], dtype=jnp.float32)[:, None]
    turb_count, elem_count = blade_coef.shape

    def forcing(state_now):
        flat_state = state_now.reshape(3, -1)
        sampled = jnp.where(owned[None], flat_state[:, flat_index], 0.0)
        beside_all = padded_2(sampled[None], (("gy", 0),), 1)
        summed = jnp.sum(beside_all, axis=0)
        velocity = (summed + wind_col).reshape(3, turb_count, elem_count)
        mean_axial = jnp.mean(velocity[0], axis=1)
        forces = (-blade_coef[None] * mean_axial[None, :, None] * velocity).reshape(3, -1)
        forces = jnp.where(owned[None], forces, 0.0)
        total = jnp.zeros_like(flat_state).at[:, flat_index].add(forces)
        return total.reshape(state_now.shape)

    def full_rate(state_now):
        padded = padded_2(state_now, (("gx", 1), ("gy", 2)), 1)
        upstream = padded[:, 0, 1:-1, :]
        from_precursor = shifted(upstream, "sec", 1)
        up_plane = jnp.where(farm_first, from_precursor, upstream)
        down_plane = jnp.where(farm_last, state_now[:, -1], padded[:, -1, 1:-1, :])
        x_plus = jnp.concatenate([state_now[:, 1:], down_plane[:, None]], axis=1)
        x_minus = jnp.concatenate([up_plane[:, None], state_now[:, :-1]], axis=1)
        y_plus = padded[:, 1:-1, 2:, :]
        y_minus = padded[:, 1:-1, :-2, :]
        vel_x = state_now[0] + wind_speed
        rates = [
            component_rate(
                state_now[c],
                x_plus[c],
                x_minus[c],
                y_plus[c],
                y_minus[c],
                vel_x,
                state_now[1],
                state_now[2],
            )
            for c in range(3)
        ]
        return jnp.stack(rates, axis=0) + forcing(state_now)

    segment_one = flow_state + time_step * full_rate(flow_state)
    segment_two = 0.75 * flow_state + 0.25 * (segment_one + time_step * full_rate(segment_one))
    return flow_state / 3.0 + 2.0 / 3.0 * (segment_two + time_step * full_rate(segment_two))


def solution(mesh):
    placed = (P(None, ("sec", "gx"), "gy", None), P(), P())
    return jax.shard_map(
        body,
        mesh=mesh,
        in_specs=placed,
        out_specs=P(None, ("sec", "gx"), "gy", None),
        check_vma=False,
    )
```

profile of v0, /device:TPU:0, one launch (start us, length us, event | category | flops | bytes accessed | tf_op | source)
XLA Modules:
  0.0 501.1 jit_solution(1432423449018636014)
XLA Ops:
  0.0 0.8 fusion.165
  0.8 9.6 %copy.48 = f32[3,8,16,256]{0,3,2,1:T(8,128)} copy(f32[3,8,16,256]{3,2,1,0:T(8,128)} %param.4) | data formatting | bytes 786432 | tf_op args[0]
  10.5 0.4 compare_select_fusion
  10.9 33.6 %gather_fusion = f32[8192,3]{1,0:T(8,128)} fusion(f32[3,32768]{0,1:T(8,128)} %bitcast.535, s32[8192]{0:T(1024)S(1)} %broadcast_clamp_fusion), kind=kCustom, calls=%fused_computation | custom fusion | bytes 229376 | tf_op jit(solution)/shard_map/gather | solution.py:63
  44.6 7.5 %bitcast_select_fusion.2 = f32[1,3,8192]{1,2,0:T(8,128)} fusion(f32[8192,3]{1,0:T(8,128)} %gather_fusion, pred[8192]{0:T(1024)(128)(4,1)S(1)} %and_and_fusion), kind=kLoop, calls=%fused_computation.17 | loop fusion | flops 24576 | bytes 204800 | tf_op jit(solution)/shard_map/jit(_where)/select_n | solution.py:63
  52.0 2.9 copy.49
  54.9 5.1 %collective-permute-start.6 = (f32[1,3,8192]{2,0,1:T(1,128)S(1)}, f32[1,3,8192]{2,0,1:T(1,128)S(1)}, u32[]{:S(2)}, u32[]{:S(2)}) collective-permute-start(f32[1,3,8192]{2,0,1:T(1,128)S(1)} %copy.49), channel_id=1, source_target_pairs={{1,0},{2,1},{3,2},{0,3},{5,4},{6,5},{7,6},{4,7},{9,8},{10,9},{11,1... | collective-permute-start | bytes 294920 | tf_op jit(solution)/shard_map/ppermute | solution.py:19
  60.0 0.7 collective-permute-start
  61.1 1.4 collective-permute-done
  62.5 1.0 collective-permute-start.1
  63.5 2.6 copy.52
  66.1 0.3 collective-permute-done.5
  66.4 2.6 copy.50
  69.1 7.5 %fusion.11 = f32[3,8192]{0,1:T(8,128)S(1)} fusion(f32[1,3,8192]{1,2,0:T(8,128)} %copy.52, f32[1,3,8192]{1,2,0:T(8,128)} %copy.50, f32[8192,3]{1,0:T(8,128)} %gather_fusion, f32[3]{0:T(128)S(1)} %copy-done.6, pred[8192]{0:T(1024)(128)(4,1)S(1)} %and_and_fusion), kind=kLoop, calls=%fused_computation.30 | loop fusion | flops 98304 | bytes 401420 | tf_op jit(solution)/shard_map/add | solution.py:66
  76.6 1.9 copy-done.1
  78.5 1.1 slice_reduce_fusion.2
  79.9 3.4 collective-permute-start.2
  83.4 69.9 %scatter_custom_fusion = f32[3,32768]{0,1:T(8,128)} fusion(s32[8192]{0:T(1024)S(1)} %bitcast.550, f32[]{:T(128)} %constant.65.clone.1, f32[3,8192]{0,1:T(8,128)} %copy-done.1, f32[8192]{0:T(1024)S(1)} %multiply_bitcast_fusion.2, pred[8192]{0:T(1024)(128)(4,1)S(1)} %and_and_fusion), kind=kCustom, calls=%fused_computation.10 | custom fusion | flops 73728 | bytes 4629504 | tf_op jit(solution)/shard_map/scatter-add | solution.py:70
  153.3 10.0 %copy.53 = f32[3,8,16,256]{3,2,1,0:T(8,128)S(1)} copy(f32[3,8,16,256]{0,3,2,1:T(8,128)} %bitcast.533) | data formatting | bytes 786432 | tf_op jit(solution)/shard_map/reshape | solution.py:71
  163.3 3.8 collective-permute-start.3
  167.2 1.6 collective-permute-done.3
  168.7 4.1 collective-permute-done.4
  172.8 0.2 fusion.120
  173.1 0.2 fusion.140
  173.4 8.6 %copy.66 = f32[3,8,16,256]{0,3,2,1:T(8,128)} copy(f32[3,8,16,256]{3,2,0,1:T(8,128)S(1)} %copy_add_fusion) | data formatting | bytes 786432 | tf_op jit(solution)/shard_map/add | solution.py:99
  182.0 33.6 %gather_fusion.1 = f32[8192,3]{1,0:T(8,128)} fusion(f32[3,32768]{0,1:T(8,128)} %bitcast.537, s32[8192]{0:T(1024)S(1)} %broadcast_clamp_fusion), kind=kCustom, calls=%fused_computation.1 | custom fusion | bytes 229376 | tf_op jit(solution)/shard_map/gather | solution.py:63
  215.7 7.5 %bitcast_select_fusion.1 = f32[1,3,8192]{1,2,0:T(8,128)} fusion(f32[8192,3]{1,0:T(8,128)} %gather_fusion.1, pred[8192]{0:T(1024)(128)(4,1)S(1)} %and_and_fusion), kind=kLoop, calls=%fused_computation.16 | loop fusion | flops 24576 | bytes 204800 | tf_op jit(solution)/shard_map/jit(_where)/select_n | solution.py:63
  223.1 2.8 copy.67
  226.0 2.0 collective-permute-start.12
  228.5 1.5 collective-permute-done.7
  230.1 1.8 collective-permute-start.8
  231.9 2.6 copy.70
  234.5 2.7 copy.68
  237.2 7.5 %fusion.9 = f32[3,8192]{0,1:T(8,128)S(1)} fusion(f32[1,3,8192]{1,2,0:T(8,128)} %copy.70, f32[1,3,8192]{1,2,0:T(8,128)} %copy.68, f32[8192,3]{1,0:T(8,128)} %gather_fusion.1, f32[3]{0:T(128)S(1)} %copy-done.6, pred[8192]{0:T(1024)(128)(4,1)S(1)} %and_and_fusion), kind=kLoop, calls=%fused_computation.25 | loop fusion | flops 98304 | bytes 401420 | tf_op jit(solution)/shard_map/add | solution.py:66
  244.7 1.9 copy-done.3
  246.6 1.1 slice_reduce_fusion.1
  247.9 1.3 collective-permute-start.9
  249.3 69.9 %scatter_custom_fusion.1 = f32[3,32768]{0,1:T(8,128)} fusion(s32[8192]{0:T(1024)S(1)} %bitcast.551, f32[]{:T(128)} %constant.65.clone.1, f32[3,8192]{0,1:T(8,128)} %copy-done.3, f32[8192]{0:T(1024)S(1)} %multiply_bitcast_fusion.1, pred[8192]{0:T(1024)(128)(4,1)S(1)} %and_and_fusion), kind=kCustom, calls=%fused_computation.8 | custom fusion | flops 73728 | bytes 4629504 | tf_op jit(solution)/shard_map/scatter-add | solution.py:70
  319.2 10.0 %copy.71 = f32[3,8,16,256]{3,2,1,0:T(8,128)S(1)} copy(f32[3,8,16,256]{0,3,2,1:T(8,128)} %bitcast.534) | data formatting | bytes 786432 | tf_op jit(solution)/shard_map/reshape | solution.py:71
  329.2 1.6 collective-permute-start.10
  330.8 0.5 collective-permute-start.11
  331.3 1.9 collective-permute-done.10
  333.1 3.4 collective-permute-done.11
  336.9 0.2 fusion.31
  337.1 8.6 %copy.74 = f32[3,8,16,256]{0,3,2,1:T(8,128)} copy(f32[3,8,16,256]{3,2,1,0:T(8,128)S(1)} %fusion.31) | data formatting | bytes 786432 | tf_op jit(solution)/shard_map/add | solution.py:100
  345.7 33.6 %gather_fusion.2 = f32[8192,3]{1,0:T(8,128)} fusion(f32[3,32768]{0,1:T(8,128)} %bitcast.536, s32[8192]{0:T(1024)S(1)} %broadcast_clamp_fusion), kind=kCustom, calls=%fused_computation.2 | custom fusion | bytes 229376 | tf_op jit(solution)/shard_map/gather | solution.py:63
  379.3 7.5 %bitcast_select_fusion = f32[1,3,8192]{1,2,0:T(8,128)} fusion(f32[8192,3]{1,0:T(8,128)} %gather_fusion.2, pred[8192]{0:T(1024)(128)(4,1)S(1)} %and_and_fusion), kind=kLoop, calls=%fused_computation.15 | loop fusion | flops 24576 | bytes 204800 | tf_op jit(solution)/shard_map/jit(_where)/select_n | solution.py:63
  386.8 2.8 copy.75
  389.7 2.0 collective-permute-start.19
  392.2 1.5 collective-permute-done.14
  393.8 1.2 collective-permute-start.15
  394.9 2.6 copy.78
  397.5 2.7 copy.76
  400.2 7.5 %fusion.7 = f32[3,8192]{0,1:T(8,128)S(1)} fusion(f32[1,3,8192]{1,2,0:T(8,128)} %copy.78, f32[1,3,8192]{1,2,0:T(8,128)} %copy.76, f32[8192,3]{1,0:T(8,128)} %gather_fusion.2, f32[3]{0:T(128)S(1)} %copy-done.6, pred[8192]{0:T(1024)(128)(4,1)S(1)} %and_and_fusion), kind=kLoop, calls=%fused_computation.20 | loop fusion | flops 98304 | bytes 401420 | tf_op jit(solution)/shard_map/add | solution.py:66
  407.7 1.9 copy-done.2
  409.7 1.1 slice_reduce_fusion
  411.0 1.3 collective-permute-start.16
  412.4 69.9 %scatter_custom_fusion.2 = f32[3,32768]{0,1:T(8,128)} fusion(s32[8192]{0:T(1024)S(1)} %bitcast.552, f32[]{:T(128)} %constant.65.clone.1, f32[3,8192]{0,1:T(8,128)} %copy-done.2, f32[8192]{0:T(1024)S(1)} %multiply_bitcast_fusion, pred[8192]{0:T(1024)(128)(4,1)S(1)} %and_and_fusion), kind=kCustom, calls=%fused_computation.6 | custom fusion | flops 73728 | bytes 4629504 | tf_op jit(solution)/shard_map/scatter-add | solution.py:70
  482.3 10.0 %copy.79 = f32[3,8,16,256]{3,2,1,0:T(8,128)S(1)} copy(f32[3,8,16,256]{0,3,2,1:T(8,128)} %bitcast.532) | data formatting | bytes 786432 | tf_op jit(solution)/shard_map/reshape | solution.py:71
  492.2 1.8 collective-permute-start.17
  494.1 0.3 collective-permute-start.18
  494.3 1.9 collective-permute-done.17
  496.2 3.6 collective-permute-done.18
  500.2 0.9 fusion.35
  (77 shorter events, 3.4 us)
Async XLA Ops:
  0.8 9.6 %copy-start.5 = (s32[3,64,128]{2,1,0:T(8,128)S(1)}, s32[3,64,128]{2,1,0:T(8,128)}, u32[]{:S(2)}) copy-start(s32[3,64,128]{2,1,0:T(8,128)} %param.5) | copy-start | bytes 294916
  52.0 8.0 %copy-start = (f32[3,8,16,256]{3,2,1,0:T(8,128)S(1)}, f32[3,8,16,256]{3,2,1,0:T(8,128)}, u32[]{:S(2)}) copy-start(f32[3,8,16,256]{3,2,1,0:T(8,128)} %param.4) | copy-start | bytes 1179652
  54.9 8.6 %collective-permute-start.6 = (f32[1,3,8192]{2,0,1:T(1,128)S(1)}, f32[1,3,8192]{2,0,1:T(1,128)S(1)}, u32[]{:S(2)}, u32[]{:S(2)}) collective-permute-start(f32[1,3,8192]{2,0,1:T(1,128)S(1)} %copy.49), channel_id=1, source_target_pairs={{1,0},{2,1},{3,2},{0,3},{5,4},{6,5},{7,6},{4,7},{9,8},{10,9},{11,1... | collective-permute-start | bytes 294920 | tf_op jit(solution)/shard_map/ppermute | solution.py:19
  60.0 6.4 %collective-permute-start.5 = (f32[1,3,8192]{2,0,1:T(1,128)S(1)}, f32[1,3,8192]{2,0,1:T(1,128)S(1)}, u32[]{:S(2)}, u32[]{:S(2)}) collective-permute-start(f32[1,3,8192]{2,0,1:T(1,128)S(1)} %copy.49), channel_id=1, source_target_pairs={{0,1},{1,2},{2,3},{3,0},{4,5},{5,6},{6,7},{7,4},{8,9},{9,10},{10,1... | collective-permute-start | bytes 294920 | tf_op jit(solution)/shard_map/ppermute | solution.py:18
  60.0 2.5 collective-permute-start
  62.5 6.6 %copy-start.6 = (f32[3]{0:T(128)S(1)}, f32[3]{0:T(128)}, u32[]{:S(2)}) copy-start(f32[3]{0:T(128)} %constant.81.clone) | copy-start | bytes 40
  62.5 17.3 %collective-permute-start.1 = (f32[3,1,16,256]{3,2,1,0:T(8,128)S(1)}, f32[3,1,16,256]{3,2,1,0:T(8,128)S(1)}, u32[]{:S(2)}, u32[]{:S(2)}) collective-permute-start(f32[3,1,16,256]{3,2,1,0:T(8,128)S(1)} %get-tuple-element.30), channel_id=1, source_target_pairs={{0,4},{4,8},{8,12},{12,0},{1,5},{5,9},{9,13},{13,1},{2,6},{6,10},{... | collective-permute-start | bytes 147464 | tf_op jit(solution)/shard_map/ppermute | solution.py:18
  76.6 1.9 copy-start.1
  78.5 4.8 copy-start.4
  79.9 87.2 %collective-permute-start.2 = (f32[3,16,256]{2,1,0:T(8,128)S(1)}, f32[3,16,256]{2,1,0:T(8,128)S(1)}, u32[]{:S(2)}, u32[]{:S(2)}) collective-permute-start(f32[3,16,256]{2,1,0:T(8,128)S(1)} %bitcast.548), channel_id=1, source_target_pairs={{0,16},{1,17},{2,18},{3,19},{4,20},{5,21},{6,22},{7,23},{8,24},{9,... | collective-permute-start | bytes 147464 | tf_op jit(solution)/shard_map/ppermute | solution.py:27
  163.3 5.4 %collective-permute-start.3 = (f32[3,10,1,256]{3,2,1,0:T(1,128)S(1)}, f32[3,10,1,256]{3,2,1,0:T(1,128)S(1)}, u32[]{:S(2)}, u32[]{:S(2)}) collective-permute-start(f32[3,10,1,256]{3,2,1,0:T(1,128)S(1)} %get-tuple-element.10), channel_id=1, source_target_pairs={{1,0},{2,1},{3,2},{0,3},{5,4},{6,5},{7,6},{4,7},{9,8},{10,9},{11,1... | collective-permute-start | bytes 92168 | tf_op jit(solution)/shard_map/ppermute | solution.py:19
  167.1 5.7 %collective-permute-start.4 = (f32[3,10,1,256]{3,2,1,0:T(1,128)S(1)}, f32[3,10,1,256]{3,2,1,0:T(1,128)S(1)}, u32[]{:S(2)}, u32[]{:S(2)}) collective-permute-start(f32[3,10,1,256]{3,2,1,0:T(1,128)S(1)} %get-tuple-element.9), channel_id=1, source_target_pairs={{0,1},{1,2},{2,3},{3,0},{4,5},{5,6},{6,7},{7,4},{8,9},{9,10},{10,1... | collective-permute-start | bytes 92168 | tf_op jit(solution)/shard_map/ppermute | solution.py:18
  225.9 5.9 %collective-permute-start.13 = (f32[1,3,8192]{2,0,1:T(1,128)S(1)}, f32[1,3,8192]{2,0,1:T(1,128)S(1)}, u32[]{:S(2)}, u32[]{:S(2)}) collective-permute-start(f32[1,3,8192]{2,0,1:T(1,128)S(1)} %copy.67), channel_id=1, source_target_pairs={{1,0},{2,1},{3,2},{0,3},{5,4},{6,5},{7,6},{4,7},{9,8},{10,9},{11,1... | collective-permute-start | bytes 294920 | tf_op jit(solution)/shard_map/ppermute | solution.py:19
  226.0 8.5 %collective-permute-start.12 = (f32[1,3,8192]{2,0,1:T(1,128)S(1)}, f32[1,3,8192]{2,0,1:T(1,128)S(1)}, u32[]{:S(2)}, u32[]{:S(2)}) collective-permute-start(f32[1,3,8192]{2,0,1:T(1,128)S(1)} %copy.67), channel_id=1, source_target_pairs={{0,1},{1,2},{2,3},{3,0},{4,5},{5,6},{6,7},{7,4},{8,9},{9,10},{10,1... | collective-permute-start | bytes 294920 | tf_op jit(solution)/shard_map/ppermute | solution.py:18
  228.3 1.8 collective-permute-start.7
  230.1 17.8 %collective-permute-start.8 = (f32[3,1,16,256]{3,2,0,1:T(8,128)S(1)}, f32[3,1,16,256]{3,2,0,1:T(8,128)S(1)}, u32[]{:S(2)}, u32[]{:S(2)}) collective-permute-start(f32[3,1,16,256]{3,2,0,1:T(8,128)S(1)} %get-tuple-element.23), channel_id=1, source_target_pairs={{0,4},{4,8},{8,12},{12,0},{1,5},{5,9},{9,13},{13,1},{2,6},{6,10},{... | collective-permute-start | bytes 147464 | tf_op jit(solution)/shard_map/ppermute | solution.py:18
  244.7 1.9 copy-start.3
  247.9 83.4 %collective-permute-start.9 = (f32[3,16,256]{2,1,0:T(8,128)S(1)}, f32[3,16,256]{2,1,0:T(8,128)S(1)}, u32[]{:S(2)}, u32[]{:S(2)}) collective-permute-start(f32[3,16,256]{2,1,0:T(8,128)S(1)} %bitcast.543), channel_id=1, source_target_pairs={{0,16},{1,17},{2,18},{3,19},{4,20},{5,21},{6,22},{7,23},{8,24},{9,... | collective-permute-start | bytes 147464 | tf_op jit(solution)/shard_map/ppermute | solution.py:27
  329.2 3.9 collective-permute-start.10
  330.8 5.7 %collective-permute-start.11 = (f32[3,10,1,256]{3,2,1,0:T(1,128)S(1)}, f32[3,10,1,256]{3,2,1,0:T(1,128)S(1)}, u32[]{:S(2)}, u32[]{:S(2)}) collective-permute-start(f32[3,10,1,256]{3,2,1,0:T(1,128)S(1)} %get-tuple-element.7), channel_id=1, source_target_pairs={{0,1},{1,2},{2,3},{3,0},{4,5},{5,6},{6,7},{7,4},{8,9},{9,10},{10,1... | collective-permute-start | bytes 92168 | tf_op jit(solution)/shard_map/ppermute | solution.py:18
  389.6 5.3 %collective-permute-start.20 = (f32[1,3,8192]{2,0,1:T(1,128)S(1)}, f32[1,3,8192]{2,0,1:T(1,128)S(1)}, u32[]{:S(2)}, u32[]{:S(2)}) collective-permute-start(f32[1,3,8192]{2,0,1:T(1,128)S(1)} %copy.75), channel_id=1, source_target_pairs={{1,0},{2,1},{3,2},{0,3},{5,4},{6,5},{7,6},{4,7},{9,8},{10,9},{11,1... | collective-permute-start | bytes 294920 | tf_op jit(solution)/shard_map/ppermute | solution.py:19
  389.7 7.9 %collective-permute-start.19 = (f32[1,3,8192]{2,0,1:T(1,128)S(1)}, f32[1,3,8192]{2,0,1:T(1,128)S(1)}, u32[]{:S(2)}, u32[]{:S(2)}) collective-permute-start(f32[1,3,8192]{2,0,1:T(1,128)S(1)} %copy.75), channel_id=1, source_target_pairs={{0,1},{1,2},{2,3},{3,0},{4,5},{5,6},{6,7},{7,4},{8,9},{9,10},{10,1... | collective-permute-start | bytes 294920 | tf_op jit(solution)/shard_map/ppermute | solution.py:18
  391.9 1.8 collective-permute-start.14
  393.8 17.3 %collective-permute-start.15 = (f32[3,1,16,256]{3,2,1,0:T(8,128)S(1)}, f32[3,1,16,256]{3,2,1,0:T(8,128)S(1)}, u32[]{:S(2)}, u32[]{:S(2)}) collective-permute-start(f32[3,1,16,256]{3,2,1,0:T(8,128)S(1)} %get-tuple-element.17), channel_id=1, source_target_pairs={{0,4},{4,8},{8,12},{12,0},{1,5},{5,9},{9,13},{13,1},{2,6},{6,10},{... | collective-permute-start | bytes 147464 | tf_op jit(solution)/shard_map/ppermute | solution.py:18
  407.7 1.9 copy-start.2
  411.0 83.3 %collective-permute-start.16 = (f32[3,16,256]{2,1,0:T(8,128)S(1)}, f32[3,16,256]{2,1,0:T(8,128)S(1)}, u32[]{:S(2)}, u32[]{:S(2)}) collective-permute-start(f32[3,16,256]{2,1,0:T(8,128)S(1)} %bitcast.542), channel_id=1, source_target_pairs={{0,16},{1,17},{2,18},{3,19},{4,20},{5,21},{6,22},{7,23},{8,24},{9,... | collective-permute-start | bytes 147464 | tf_op jit(solution)/shard_map/ppermute | solution.py:27
  492.2 3.9 collective-permute-start.17
  494.1 5.7 %collective-permute-start.18 = (f32[3,10,1,256]{3,2,1,0:T(1,128)S(1)}, f32[3,10,1,256]{3,2,1,0:T(1,128)S(1)}, u32[]{:S(2)}, u32[]{:S(2)}) collective-permute-start(f32[3,10,1,256]{3,2,1,0:T(1,128)S(1)} %get-tuple-element.5), channel_id=1, source_target_pairs={{0,1},{1,2},{2,3},{3,0},{4,5},{5,6},{6,7},{7,4},{8,9},{9,10},{10,1... | collective-permute-start | bytes 92168 | tf_op jit(solution)/shard_map/ppermute | solution.py:18
where the time goes:
time: 503 us; the launch traced here: 501 us
  other arithmetic  258 us (51%)
  local copies, waits for them, and re-layouts  193 us (38%)
  starting transfers between devices  28.1 us (6%)
  waiting for transfers between devices  21.1 us (4%)
    scatter-add x3, other arithmetic, forcing(): total = jnp.zeros_like(flat_state).at[:, flat_index].add(forces)  210 us
    gather x3, local copies, waits for them, and re-layouts, forcing(): sampled = jnp.where(owned[None], flat_state[:, flat_index], 0.0)  101 us
    reshape x3, local copies, waits for them, and re-layouts, forcing(): return total.reshape(state_now.shape)  29.9 us
    add x3, other arithmetic, forcing(): velocity = (summed + wind_col).reshape(3, turb_count, elem_count)  22.5 us
    select_n x3, other arithmetic, forcing(): sampled = jnp.where(owned[None], flat_state[:, flat_index], 0.0)  22.4 us
    unnamed x17, local copies, waits for them, and re-layouts  15.4 us
    ppermute x9, starting transfers between devices, padded_2(): after = lax.ppermute(initial, axis, down)  13.3 us
    ppermute x9, waiting for transfers between devices, padded_2(): before = lax.ppermute(last, axis, up)  11.3 us
  transfers between devices with their start and end apart: 21, of which 10 were waited for; matrix products, arithmetic and copies ran while one was open for 57% of the time, Pallas kernels for 0%

commit v1 on v0

v1 whole, which is shorter than its diff:
```python
import functools

import jax
import jax.numpy as jnp
from jax import lax
from jax.experimental import pallas as pl
from jax.experimental.pallas import tpu as pltpu
from jax.sharding import PartitionSpec as P

time_step = 0.3
viscosity = 0.1
wind_speed = 1.0
MESH = pl.DeviceIdType.MESH
STAGES = ((0.0, 1.0, time_step), (0.75, 0.25, 0.25 * time_step), (1.0 / 3.0, 2.0 / 3.0, 2.0 / 3.0 * time_step))


def footprints_kernel(plane_ref, cells_ref, coef_ref, count_ref, weight_ref):
    turb_count, rows_y, rows_z = count_ref.shape
    points = coef_ref.shape[1]
    first_row = lax.axis_index("gy") * rows_y

    def one(t, carry):
        @pl.when(plane_ref[t] >= 0)
        def _():
            y = cells_ref[1, pl.ds(t, 1), :] - first_row
            z = cells_ref[2, pl.ds(t, 1), :]
            coef = coef_ref[pl.ds(t, 1), :]
            hi = coef.astype(jnp.bfloat16).astype(jnp.float32)
            mid = (coef - hi).astype(jnp.bfloat16).astype(jnp.float32)
            low = coef - hi - mid
            in_row = lax.broadcasted_iota(jnp.int32, (rows_y, points), 0) == y
            left = jnp.concatenate(
                [jnp.where(in_row, part, 0.0) for part in (jnp.full_like(coef, 1.0 / points), hi, mid, low)], axis=0
            ).astype(jnp.bfloat16)
            right = jnp.where(lax.broadcasted_iota(jnp.int32, (rows_z, points), 0) == z, 1.0, 0.0).astype(jnp.bfloat16)
            both = lax.dot_general(left, right, (((1,), (1,)), ((), ())), preferred_element_type=jnp.float32)
            count_ref[t] = both[:rows_y]
            weight_ref[t] = -(both[rows_y : 2 * rows_y] + (both[2 * rows_y : 3 * rows_y] + both[3 * rows_y :]))

        @pl.when(plane_ref[t] < 0)
        def _():
            count_ref[t] = jnp.zeros((rows_y, rows_z), jnp.float32)
            weight_ref[t] = jnp.zeros((rows_y, rows_z), jnp.float32)

        return carry

    lax.fori_loop(0, turb_count, one, 0)


def flow_kernel(
    slabs, spans,
    plane_ref, start_ref, cells_ref, count_ref, weight_ref, out_ref,
    one_ref, two_ref, acc_ref, drag_ref, part_ref, mean_ref,
    y_out, y_in, x_in, send_sem, recv_sem,
):
    n_comp, rows_x, rows_y, rows_z = start_ref.shape
    turb_count, half = part_ref.shape
    sec, slab, span = lax.axis_index("sec"), lax.axis_index("gx"), lax.axis_index("gy")
    in_farm = sec == 1
    has_left = jnp.logical_or(sec == 0, slab > 0)
    has_right = jnp.logical_or(sec == 0, slab < slabs - 1)
    farm_last = jnp.logical_and(in_farm, slab == slabs - 1)
    prec_last = jnp.logical_and(sec == 0, slab == slabs - 1)
    farm_first = jnp.logical_and(in_farm, slab == 0)
    right = (sec, lax.rem(slab + 1, slabs), span)
    left = (sec, lax.rem(slab + slabs - 1, slabs), span)
    above = (sec, slab, lax.rem(span + 1, spans))
    below = (sec, slab, lax.rem(span + spans - 1, spans))
    to_farm = (1, 0, span)
    to_prec = (0, slabs - 1, span)

    barrier = pltpu.get_barrier_semaphore()
    partners = ((above, None), (below, None), (right, has_right), (left, has_left), (to_farm, prec_last), (to_prec, farm_first))
    for device, when in partners:
        def greet(device=device):
            pl.semaphore_signal(barrier, inc=1, device_id=device, device_id_type=MESH)
        greet() if when is None else pl.when(when)(greet)
    peers = 2
    for _, when in partners[2:]:
        peers = peers + jnp.where(when, 1, 0)
    pl.semaphore_wait(barrier, peers)

    row = lax.broadcasted_iota(jnp.int32, (rows_y, rows_z), 0)
    col = lax.broadcasted_iota(jnp.int32, (rows_y, rows_z), 1)
    low_row, high_row = row == 0, row == rows_y - 1
    low_col, high_col = col == 0, col == rows_z - 1
    diagonal = lax.broadcasted_iota(jnp.int32, (turb_count, half), 0) == lax.broadcasted_iota(jnp.int32, (turb_count, half), 1)
    lines = n_comp * rows_x

    states = (start_ref, one_ref, two_ref, out_ref)
    for stage, (keep, here, step) in enumerate(STAGES):
        now, later = states[stage], states[stage + 1]

        def remote(src, dst, s, r, device):
            return pltpu.make_async_remote_copy(
                src_ref=src, dst_ref=dst, send_sem=send_sem.at[stage, s], recv_sem=recv_sem.at[stage, r],
                device_id=device, device_id_type=MESH,
            )

        go_right = remote(now.at[:, rows_x - 1], x_in.at[stage, 0], 0, 0, right)
        go_left = remote(now.at[:, 0], x_in.at[stage, 1], 1, 1, left)
        go_farm = remote(now.at[:, rows_x - 1], x_in.at[stage, 0], 2, 0, to_farm)
        go_above = remote(y_out.at[stage, 0], y_in.at[stage, 0], 3, 2, above)
        go_below = remote(y_out.at[stage, 1], y_in.at[stage, 1], 4, 3, below)
        pl.when(has_right)(go_right.start)
        pl.when(has_left)(go_left.start)
        pl.when(prec_last)(go_farm.start)

        @pl.when(farm_last)
        def _():
            x_in[stage, 1] = now[:, rows_x - 1]

        @pl.when(in_farm)
        def _():
            def eight(i, carry):
                for k in range(8):
                    t = i * 8 + k
                    p = count_ref[t] * now[0, jnp.maximum(plane_ref[t], 0)]
                    p = p[:, :half] + p[:, half:]
                    part_ref[pl.ds(t, 1), :] = jnp.sum(p, axis=0, keepdims=True)
                return carry

            lax.fori_loop(0, turb_count // 8, eight, 0)
            sums = jnp.sum(part_ref[...], axis=1, keepdims=True)
            sums = jnp.sum(jnp.where(diagonal, sums, 0.0), axis=0, keepdims=True)
            for side in range(2):
                y_out[stage, side, pl.ds(lines, 1), pl.ds(0, half)] = sums

        for c in range(n_comp):
            for x in range(rows_x):
                y_out[stage, 0, pl.ds(c * rows_x + x, 1), :] = now[c, x, pl.ds(rows_y - 1, 1), :]
                y_out[stage, 1, pl.ds(c * rows_x + x, 1), :] = now[c, x, pl.ds(0, 1), :]
        go_above.start()
        go_below.start()

        for x in range(rows_x):
            v0 = (now[0, x] + wind_speed) * -0.5
            v1 = now[1, x] * -0.5
            v2 = now[2, x] * -0.5
            for c in range(n_comp):
                q = now[c, x]
                y_plus = jnp.where(high_row, 0.0, pltpu.roll(q, rows_y - 1, 0))
                y_minus = jnp.where(low_row, 0.0, pltpu.roll(q, 1, 0))
                z_plus = jnp.where(high_col, 0.0, pltpu.roll(q, rows_z - 1, 1))
                z_minus = jnp.where(low_col, 0.0, pltpu.roll(q, 1, 1))
                rate = v1 * (y_plus - y_minus) + v2 * (z_plus - z_minus)
                around = (y_plus + y_minus) + (z_plus + z_minus) - 6.0 * q
                if x == 0:
                    x_plus = now[c, x + 1]
                    rate, around = rate + v0 * x_plus, around + x_plus
                elif x == rows_x - 1:
                    x_minus = now[c, x - 1]
                    rate, around = rate - v0 * x_minus, around + x_minus
                else:
                    x_plus, x_minus = now[c, x + 1], now[c, x - 1]
                    rate, around = rate + v0 * (x_plus - x_minus), around + (x_plus + x_minus)
                total = here * q + step * (rate + viscosity * around)
                if keep:
                    total = total + keep * start_ref[c, x]
                acc_ref[c, x] = total

        go_above.wait_recv()
        go_below.wait_recv()

        @pl.when(in_farm)
        def _():
            sums = y_out[stage, 0, pl.ds(lines, 1), pl.ds(0, half)]
            for side in range(2):
                sums = sums + y_in[stage, side, pl.ds(lines, 1), pl.ds(0, half)]
            mean = jnp.sum(jnp.where(diagonal, sums, 0.0), axis=1, keepdims=True) + wind_speed
            first = slab * rows_x
            for x in range(rows_x):
                masked = jnp.where(cells_ref[0] == first + x, mean, 0.0)
                mean_ref[x, :, pl.ds(0, half)] = masked
                mean_ref[x, :, pl.ds(half, half)] = masked

            def one(t, drags):
                w = weight_ref[t]
                return tuple(d + w * mean_ref[x, pl.ds(t, 1), :] for x, d in enumerate(drags))

            zero = jnp.zeros((rows_y, rows_z), jnp.float32)
            drags = lax.fori_loop(0, turb_count, one, (zero,) * rows_x)
            for x in range(rows_x):
                drag_ref[x] = drags[x]

        @pl.when(jnp.logical_not(in_farm))
        def _():
            drag_ref[...] = jnp.zeros_like(drag_ref)

        go_right.wait_recv()
        pl.when(has_right)(go_left.wait_recv)

        for x in range(rows_x):
            q = [now[c, x] for c in range(n_comp)]
            drag = drag_ref[x]
            y_scale = viscosity + jnp.where(low_row, 0.5, -0.5) * q[1]
            for c in range(n_comp):
                line = pl.ds(c * rows_x + x, 1)
                beside = jnp.where(low_row, y_in[stage, 0, line, :], jnp.where(high_row, y_in[stage, 1, line, :], 0.0))
                rate = beside * y_scale + drag * (q[c] + wind_speed if c == 0 else q[c])
                if x == 0:
                    rate = rate + x_in[stage, 0, c] * (viscosity + 0.5 * (q[0] + wind_speed))
                if x == rows_x - 1:
                    rate = rate + x_in[stage, 1, c] * (viscosity - 0.5 * (q[0] + wind_speed))
                later[c, x] = acc_ref[c, x] + step * rate

        pl.when(has_right)(go_right.wait_send)
        pl.when(has_left)(go_left.wait_send)
        pl.when(prec_last)(go_farm.wait_send)
        go_above.wait_send()
        go_below.wait_send()


def body(slabs, spans, flow_state, blade_cells, blade_coef):
    n_comp, rows_x, rows_y, rows_z = flow_state.shape
    turb_count, points = blade_coef.shape
    half = rows_z // 2
    plane = blade_cells[0, :, 0] - lax.axis_index("gx") * rows_x
    row = blade_cells[1] - lax.axis_index("gy") * rows_y
    near = jnp.any(jnp.logical_and(row >= 0, row < rows_y), axis=1)
    near = jnp.logical_and(near, jnp.logical_and(plane >= 0, plane < rows_x))
    plane = jnp.where(jnp.logical_and(near, lax.axis_index("sec") == 1), plane, -1)
    smem = pl.BlockSpec(memory_space=pltpu.SMEM)
    vmem = pl.BlockSpec(memory_space=pltpu.VMEM)
    foot = jax.ShapeDtypeStruct((turb_count, rows_y, rows_z), jnp.float32)
    count, weight = pl.pallas_call(
        footprints_kernel,
        out_shape=(foot, foot),
        in_specs=[smem, vmem, vmem],
        out_specs=(vmem, vmem),
        compiler_params=pltpu.CompilerParams(vmem_limit_bytes=16 << 20),
        name="footprints",
    )(plane, blade_cells, blade_coef)
    block = pltpu.VMEM(flow_state.shape, jnp.float32)
    lines = (n_comp * rows_x + 1 + 7) // 8 * 8
    return pl.pallas_call(
        functools.partial(flow_kernel, slabs, spans),
        out_shape=jax.ShapeDtypeStruct(flow_state.shape, jnp.float32),
        in_specs=[smem, vmem, vmem, vmem, vmem],
        out_specs=vmem,
        scratch_shapes=[
            block, block, block,
            pltpu.VMEM((rows_x, rows_y, rows_z), jnp.float32),
            pltpu.VMEM((turb_count, half), jnp.float32),
            pltpu.VMEM((rows_x, turb_count, rows_z), jnp.float32),
            pltpu.VMEM((3, 2, lines, rows_z), jnp.float32),
            pltpu.VMEM((3, 2, lines, rows_z), jnp.float32),
            pltpu.VMEM((3, 2, n_comp, rows_y, rows_z), jnp.float32),
            pltpu.SemaphoreType.DMA((3, 5)),
            pltpu.SemaphoreType.DMA((3, 4)),
        ],
        compiler_params=pltpu.CompilerParams(
            collective_id=0, has_side_effects=True, vmem_limit_bytes=32 << 20
        ),
        name="substeps",
    )(plane, flow_state, blade_cells, count, weight)


def solution(mesh):
    placed = (P(None, ("sec", "gx"), "gy", None), P(), P())
    return jax.shard_map(
        functools.partial(body, mesh.shape["gx"], mesh.shape["gy"]),
        mesh=mesh,
        in_specs=placed,
        out_specs=P(None, ("sec", "gx"), "gy", None),
        check_vma=False,
    )
```

time: 503 us -> 29.2 us (0.06)
  the two profiles are of different devices: /device:TPU:0 before, /device:TPU:4 now
where the time goes in v1:
time: 29.2 us; the launch traced here: 28.9 us
  Pallas kernels  24.4 us (84%)
  local copies, waits for them, and re-layouts  2.63 us (9%)
  other arithmetic  1.76 us (6%)
    pallas_call x1, Pallas kernels, body(): pl.pallas_call(functools.partial(flow_kernel, slabs, spans), out_shape=ja...  21.2 us
    pallas_call x1, Pallas kernels, body(): pl.pallas_call(footprints_kernel, out_shape=(foot, foot), in_specs=[smem,...  3.2 us
    unnamed x9, local copies, waits for them, and re-layouts  2.63 us
    reduce_or x1, other arithmetic, body(): near = jnp.any(jnp.logical_and(row >= 0, row < rows_y), axis=1)  0.88 us
    sub x1, other arithmetic, body(): plane = blade_cells[0, :, 0] - lax.axis_index('gx') * rows_x  0.87 us

profile of v1, /device:TPU:4, one launch (start us, length us, event | category | flops | bytes accessed | tf_op | source)
XLA Modules:
  0.0 28.9 jit_solution(10856610878652556572)
XLA Ops:
  0.0 0.0 copy-start.3
  0.0 0.9 %subtract_reduce_fusion = s32[64]{0:T(128)S(1)} fusion(s32[3,64,128]{2,1,0:T(8,128)} %cells_ref.3, s32[]{:T(128)S(6)} %mul.7), kind=kLoop, calls=%fused_computation | loop fusion | flops 64 | bytes 516 | tf_op jit(solution)/shard_map/sub | solution.py:218
  0.9 0.9 %and_reduce_fusion = pred[64]{0:T(512)(128)(4,1)S(1)} fusion(s32[3,64,128]{2,1,0:T(8,128)} %cells_ref.3, s32[]{:T(128)S(6)} %mul.6), kind=kLoop, calls=%fused_computation.2 | loop fusion | flops 40896 | bytes 32836 | tf_op jit(solution)/shard_map/reduce_or | solution.py:220
  1.8 0.0 copy-done.3
  1.8 0.0 copy-start
  1.8 0.9 %copy-done = s32[3,64,128]{2,1,0:T(8,128)S(1)} copy-done((s32[3,64,128]{2,1,0:T(8,128)S(1)}, s32[3,64,128]{2,1,0:T(8,128)}, u32[]{:S(2)}) %copy-start) | copy-done | bytes 98328
  2.7 0.0 copy-start.1
  2.7 3.2 %footprints.1 = (f32[64,16,256]{2,1,0:T(8,128)S(1)}, f32[64,16,256]{2,1,0:T(8,128)S(1)}) custom-call(s32[64]{0:T(128)S(1)} %and_select_fusion.plane_ref, s32[3,64,128]{2,1,0:T(8,128)S(1)} %copy-done, f32[64,128]{1,0:T(8,128)S(1)} %copy-done.3), custom_call_target="tpu_custom_call" | custom-call | tf_op jit(solution)/shard_map/footprints/pallas_call | solution.py:226
  5.9 0.0 copy-done.1
  5.9 0.0 copy-start.2
  5.9 1.0 %copy-done.2 = f32[3,8,16,256]{3,2,1,0:T(8,128)S(1)} copy-done((f32[3,8,16,256]{3,2,1,0:T(8,128)S(1)}, f32[3,8,16,256]{3,2,1,0:T(8,128)}, u32[]{:S(2)}) %copy-start.2) | copy-done | bytes 393240
  6.9 21.2 %substeps.1 = f32[3,8,16,256]{3,2,1,0:T(8,128)S(1)} custom-call(s32[64]{0:T(128)S(1)} %and_select_fusion.plane_ref, f32[3,8,16,256]{3,2,1,0:T(8,128)S(1)} %copy-done.2, s32[3,64,128]{2,1,0:T(8,128)S(1)} %copy-done.1, f32[64,16,256]{2,1,0:T(8,128)S(1)} %get-tuple-element.7.count_ref, f32[64,16,256]{2,1,0:T(8,128)S(1)} %get-tuple-element.8.weight_ref), custom_call_target="tpu_custom_call" | custom-call | tf_op jit(solution)/shard_map/substeps/pallas_call | solution.py:236
  28.1 0.7 %copy.5 = f32[3,8,16,256]{3,2,1,0:T(8,128)} copy(f32[3,8,16,256]{3,2,1,0:T(8,128)S(1)} %substeps.1) | data formatting | bytes 786432
  (1 shorter events, 0.0 us)
Async XLA Ops:
  0.0 1.8 %copy-start.3 = (f32[64,128]{1,0:T(8,128)S(1)}, f32[64,128]{1,0:T(8,128)}, u32[]{:S(2)}) copy-start(f32[64,128]{1,0:T(8,128)} %coef_ref.1) | copy-start | bytes 98308
  1.8 0.9 %copy-start = (s32[3,64,128]{2,1,0:T(8,128)S(1)}, s32[3,64,128]{2,1,0:T(8,128)}, u32[]{:S(2)}) copy-start(s32[3,64,128]{2,1,0:T(8,128)} %cells_ref.3) | copy-start | bytes 294916
  2.7 3.2 %copy-start.1 = (s32[3,64,128]{2,1,0:T(8,128)S(1)}, s32[3,64,128]{2,1,0:T(8,128)}, u32[]{:S(2)}) copy-start(s32[3,64,128]{2,1,0:T(8,128)} %cells_ref.3) | copy-start | bytes 294916
  5.9 1.0 %copy-start.2 = (f32[3,8,16,256]{3,2,1,0:T(8,128)S(1)}, f32[3,8,16,256]{3,2,1,0:T(8,128)}, u32[]{:S(2)}) copy-start(f32[3,8,16,256]{3,2,1,0:T(8,128)} %start_ref.1) | copy-start | bytes 1179652

commit v2 on v1

--- a/solution.py
+++ b/solution.py
@@ -14,14 +14,56 @@
 STAGES = ((0.0, 1.0, time_step), (0.75, 0.25, 0.25 * time_step), (1.0 / 3.0, 2.0 / 3.0, 2.0 / 3.0 * time_step))
 
 
-def footprints_kernel(plane_ref, cells_ref, coef_ref, count_ref, weight_ref):
+def footprints_kernel(cells_hbm, coef_hbm, count_ref, weight_ref, table_ref, cells_ref, coef_ref, heads_ref, head_ref, last_ref, link_ref, sems):
     turb_count, rows_y, rows_z = count_ref.shape
+    rows_x = last_ref.shape[0]
     points = coef_ref.shape[1]
-    first_row = lax.axis_index("gy") * rows_y
-
-    def one(t, carry):
-        @pl.when(plane_ref[t] >= 0)
-        def _():
+
+    for i in range(3 * turb_count):
+        table_ref[i] = 0
+    for x in range(rows_x):
+        table_ref[3 * turb_count + x] = turb_count
+        last_ref[x] = -1
+
+    @pl.when(lax.axis_index("sec") == 1)
+    def _():
+        get_cells = pltpu.make_async_copy(cells_hbm, cells_ref, sems.at[0])
+        get_coef = pltpu.make_async_copy(coef_hbm, coef_ref, sems.at[1])
+        get_cells.start()
+        get_coef.start()
+        count_ref[...] = jnp.zeros_like(count_ref)
+        get_cells.wait()
+        diagonal = lax.broadcasted_iota(jnp.int32, (turb_count, points), 0) == lax.broadcasted_iota(jnp.int32, (turb_count, points), 1)
+        for i in range(2):
+            heads_ref[pl.ds(i, 1), :] = jnp.sum(jnp.where(diagonal, cells_ref[i], 0), axis=0, keepdims=True)
+        to_scalars = pltpu.make_async_copy(heads_ref, head_ref, sems.at[2])
+        to_scalars.start()
+        spans = lax.axis_size("gy")
+        span = lax.axis_index("gy")
+        first_row = span * rows_y
+        first_plane = lax.axis_index("gx") * rows_x
+        to_scalars.wait()
+        get_coef.wait()
+
+        def chain(t, carry):
+            plane = head_ref[0, t] - first_plane
+            border = lax.div(head_ref[1, t] + rows_y // 2, rows_y)
+            above = jnp.where(border == spans, 0, border)
+            inside = jnp.logical_and(plane >= 0, plane < rows_x)
+            near = jnp.logical_and(inside, jnp.logical_or(above == span, border - 1 == span))
+            near = jnp.logical_or(near, jnp.logical_and(inside, jnp.logical_and(border == 0, span == spans - 1)))
+
+            @pl.when(near)
+            def _():
+                table_ref[t] = plane
+                link_ref[t] = last_ref[plane]
+                last_ref[plane] = t
+
+            return carry
+
+        lax.fori_loop(0, turb_count, chain, 0)
+
+        def footprint(t, slot):
             y = cells_ref[1, pl.ds(t, 1), :] - first_row
             z = cells_ref[2, pl.ds(t, 1), :]
             coef = coef_ref[pl.ds(t, 1), :]
@@ -35,23 +77,30 @@
             right = jnp.where(lax.broadcasted_iota(jnp.int32, (rows_z, points), 0) == z, 1.0, 0.0).astype(jnp.bfloat16)
             both = lax.dot_general(left, right, (((1,), (1,)), ((), ())), preferred_element_type=jnp.float32)
             count_ref[t] = both[:rows_y]
-            weight_ref[t] = -(both[rows_y : 2 * rows_y] + (both[2 * rows_y : 3 * rows_y] + both[3 * rows_y :]))
-
-        @pl.when(plane_ref[t] < 0)
-        def _():
-            count_ref[t] = jnp.zeros((rows_y, rows_z), jnp.float32)
-            weight_ref[t] = jnp.zeros((rows_y, rows_z), jnp.float32)
-
-        return carry
-
-    lax.fori_loop(0, turb_count, one, 0)
+            weight_ref[slot] = -(both[rows_y : 2 * rows_y] + (both[2 * rows_y : 3 * rows_y] + both[3 * rows_y :]))
+
+        def one_plane(x, slot):
+            def more(state):
+                return state[0] >= 0
+
+            def one(state):
+                t, k = state
+                footprint(t, k)
+                table_ref[turb_count + k] = t
+                table_ref[2 * turb_count + k] = jnp.where(k == slot, 0, 1)
+                table_ref[3 * turb_count + x] = k
+                return link_ref[t], k + 1
+
+            return lax.while_loop(more, one, (last_ref[x], slot))[1]
+
+        lax.fori_loop(0, rows_x, one_plane, 0)
 
 
 def flow_kernel(
     slabs, spans,
-    plane_ref, start_ref, cells_ref, count_ref, weight_ref, out_ref,
-    one_ref, two_ref, acc_ref, drag_ref, part_ref, mean_ref,
-    y_out, y_in, x_in, send_sem, recv_sem,
+    table_ref, start_hbm, count_ref, weight_ref, out_ref,
+    start_ref, one_ref, two_ref, acc_ref, drag_ref, part_ref, mean_ref,
+    y_out, y_in, x_in, sums_out, sums_in, send_sem, recv_sem, load_sem,
 ):
     n_comp, rows_x, rows_y, rows_z = start_ref.shape
     turb_count, half = part_ref.shape
@@ -69,6 +118,8 @@
     to_farm = (1, 0, span)
     to_prec = (0, slabs - 1, span)
 
+    load = pltpu.make_async_copy(start_hbm, start_ref, load_sem)
+    load.start()
     barrier = pltpu.get_barrier_semaphore()
     partners = ((above, None), (below, None), (right, has_right), (left, has_left), (to_farm, prec_last), (to_prec, farm_first))
     for device, when in partners:
@@ -78,14 +129,14 @@
     peers = 2
     for _, when in partners[2:]:
         peers = peers + jnp.where(when, 1, 0)
-    pl.semaphore_wait(barrier, peers)
+    drag_ref[turb_count] = jnp.zeros((rows_y, rows_z), jnp.float32)
+    load.wait()
 
     row = lax.broadcasted_iota(jnp.int32, (rows_y, rows_z), 0)
     col = lax.broadcasted_iota(jnp.int32, (rows_y, rows_z), 1)
     low_row, high_row = row == 0, row == rows_y - 1
     low_col, high_col = col == 0, col == rows_z - 1
     diagonal = lax.broadcasted_iota(jnp.int32, (turb_count, half), 0) == lax.broadcasted_iota(jnp.int32, (turb_count, half), 1)
-    lines = n_comp * rows_x
 
     states = (start_ref, one_ref, two_ref, out_ref)
     for stage, (keep, here, step) in enumerate(STAGES):
@@ -102,20 +153,26 @@
         go_farm = remote(now.at[:, rows_x - 1], x_in.at[stage, 0], 2, 0, to_farm)
         go_above = remote(y_out.at[stage, 0], y_in.at[stage, 0], 3, 2, above)
         go_below = remote(y_out.at[stage, 1], y_in.at[stage, 1], 4, 3, below)
+        sums_above = remote(sums_out.at[stage], sums_in.at[stage, 0], 5, 4, above)
+        sums_below = remote(sums_out.at[stage], sums_in.at[stage, 1], 6, 5, below)
+        for c in range(n_comp):
+            for x in range(rows_x):
+                y_out[stage, 0, pl.ds(c * rows_x + x, 1), :] = now[c, x, pl.ds(rows_y - 1, 1), :]
+                y_out[stage, 1, pl.ds(c * rows_x + x, 1), :] = now[c, x, pl.ds(0, 1), :]
+        if stage == 0:
+            pl.semaphore_wait(barrier, peers)
+        go_above.start()
+        go_below.start()
         pl.when(has_right)(go_right.start)
         pl.when(has_left)(go_left.start)
         pl.when(prec_last)(go_farm.start)
-
-        @pl.when(farm_last)
-        def _():
-            x_in[stage, 1] = now[:, rows_x - 1]
 
         @pl.when(in_farm)
         def _():
             def eight(i, carry):
                 for k in range(8):
                     t = i * 8 + k
-                    p = count_ref[t] * now[0, jnp.maximum(plane_ref[t], 0)]
+                    p = count_ref[t] * now[0, table_ref[t]]
                     p = p[:, :half] + p[:, half:]
                     part_ref[pl.ds(t, 1), :] = jnp.sum(p, axis=0, keepdims=True)
                 return carry
@@ -123,15 +180,13 @@
             lax.fori_loop(0, turb_count // 8, eight, 0)
             sums = jnp.sum(part_ref[...], axis=1, keepdims=True)
             sums = jnp.sum(jnp.where(diagonal, sums, 0.0), axis=0, keepdims=True)
-            for side in range(2):
-                y_out[stage, side, pl.ds(lines, 1), pl.ds(0, half)] = sums
-
-        for c in range(n_comp):
-            for x in range(rows_x):
-                y_out[stage, 0, pl.ds(c * rows_x + x, 1), :] = now[c, x, pl.ds(rows_y - 1, 1), :]
-                y_out[stage, 1, pl.ds(c * rows_x + x, 1), :] = now[c, x, pl.ds(0, 1), :]
-        go_above.start()
-        go_below.start()
+            sums_out[stage] = jnp.broadcast_to(sums, sums_out.shape[1:])
+            sums_above.start()
+            sums_below.start()
+
+        @pl.when(farm_last)
+        def _():
+            x_in[stage, 1] = now[:, rows_x - 1]
 
         for x in range(rows_x):
             v0 = (now[0, x] + wind_speed) * -0.5
@@ -159,40 +214,33 @@
                     total = total + keep * start_ref[c, x]
                 acc_ref[c, x] = total
 
+        @pl.when(in_farm)
+        def _():
+            sums_above.wait_recv()
+            sums_below.wait_recv()
+            sums = sums_out[stage, pl.ds(0, 1), :] + sums_in[stage, 0, pl.ds(0, 1), :] + sums_in[stage, 1, pl.ds(0, 1), :]
+            mean = jnp.sum(jnp.where(diagonal, sums, 0.0), axis=1, keepdims=True) + wind_speed
+            mean_ref[...] = jnp.broadcast_to(mean, mean_ref.shape)
+
+            def eight_slots(i, acc):
+                for k in range(8):
+                    slot = i * 8 + k
+                    scale = mean_ref[pl.ds(table_ref[turb_count + slot], 1), :]
+                    force = weight_ref[slot] * jnp.concatenate([scale, scale], axis=1)
+                    acc = jnp.where(table_ref[2 * turb_count + slot] > 0, acc, 0.0) + force
+                    drag_ref[slot] = acc
+                return acc
+
+            lax.fori_loop(0, turb_count // 8, eight_slots, jnp.zeros((rows_y, rows_z), jnp.float32))
+
         go_above.wait_recv()
         go_below.wait_recv()
-
-        @pl.when(in_farm)
-        def _():
-            sums = y_out[stage, 0, pl.ds(lines, 1), pl.ds(0, half)]
-            for side in range(2):
-                sums = sums + y_in[stage, side, pl.ds(lines, 1), pl.ds(0, half)]
-            mean = jnp.sum(jnp.where(diagonal, sums, 0.0), axis=1, keepdims=True) + wind_speed
-            first = slab * rows_x
-            for x in range(rows_x):
-                masked = jnp.where(cells_ref[0] == first + x, mean, 0.0)
-                mean_ref[x, :, pl.ds(0, half)] = masked
-                mean_ref[x, :, pl.ds(half, half)] = masked
-
-            def one(t, drags):
-                w = weight_ref[t]
-                return tuple(d + w * mean_ref[x, pl.ds(t, 1), :] for x, d in enumerate(drags))
-
-            zero = jnp.zeros((rows_y, rows_z), jnp.float32)
-            drags = lax.fori_loop(0, turb_count, one, (zero,) * rows_x)
-            for x in range(rows_x):
-                drag_ref[x] = drags[x]
-
-        @pl.when(jnp.logical_not(in_farm))
-        def _():
-            drag_ref[...] = jnp.zeros_like(drag_ref)
-
         go_right.wait_recv()
         pl.when(has_right)(go_left.wait_recv)
 
         for x in range(rows_x):
             q = [now[c, x] for c in range(n_comp)]
-            drag = drag_ref[x]
+            drag = drag_ref[table_ref[3 * turb_count + x]]
             y_scale = viscosity + jnp.where(low_row, 0.5, -0.5) * q[1]
             for c in range(n_comp):
                 line = pl.ds(c * rows_x + x, 1)
@@ -209,51 +257,62 @@
         pl.when(prec_last)(go_farm.wait_send)
         go_above.wait_send()
         go_below.wait_send()
+        pl.when(in_farm)(sums_above.wait_send)
+        pl.when(in_farm)(sums_below.wait_send)
 
 
 def body(slabs, spans, flow_state, blade_cells, blade_coef):
     n_comp, rows_x, rows_y, rows_z = flow_state.shape
     turb_count, points = blade_coef.shape
     half = rows_z // 2
-    plane = blade_cells[0, :, 0] - lax.axis_index("gx") * rows_x
-    row = blade_cells[1] - lax.axis_index("gy") * rows_y
-    near = jnp.any(jnp.logical_and(row >= 0, row < rows_y), axis=1)
-    near = jnp.logical_and(near, jnp.logical_and(plane >= 0, plane < rows_x))
-    plane = jnp.where(jnp.logical_and(near, lax.axis_index("sec") == 1), plane, -1)
     smem = pl.BlockSpec(memory_space=pltpu.SMEM)
     vmem = pl.BlockSpec(memory_space=pltpu.VMEM)
+    hbm = pl.BlockSpec(memory_space=pltpu.HBM)
     foot = jax.ShapeDtypeStruct((turb_count, rows_y, rows_z), jnp.float32)
-    count, weight = pl.pallas_call(
+    count, weight, table = pl.pallas_call(
         footprints_kernel,
-        out_shape=(foot, foot),
-        in_specs=[smem, vmem, vmem],
-        out_specs=(vmem, vmem),
+        out_shape=(foot, foot, jax.ShapeDtypeStruct((3 * turb_count + rows_x,), jnp.int32)),
+        in_specs=[hbm, hbm],
+        out_specs=(vmem, vmem, smem),
+        scratch_shapes=[
+            pltpu.VMEM(blade_cells.shape, jnp.int32),
+            pltpu.VMEM(blade_coef.shape, jnp.float32),
+            pltpu.VMEM((8, points), jnp.int32),
+            pltpu.SMEM((8, points), jnp.int32),
+            pltpu.SMEM((rows_x,), jnp.int32),
+            pltpu.SMEM((turb_count,), jnp.int32),
+            pltpu.SemaphoreType.DMA((3,)),
+        ],
         compiler_params=pltpu.CompilerParams(vmem_limit_bytes=16 << 20),
+        cost_estimate=pl.CostEstimate(flops=4 << 30, bytes_accessed=16 << 20, transcendentals=0),
         name="footprints",
-    )(plane, blade_cells, blade_coef)
+    )(blade_cells, blade_coef)
     block = pltpu.VMEM(flow_state.shape, jnp.float32)
-    lines = (n_comp * rows_x + 1 + 7) // 8 * 8
+    lines = (n_comp * rows_x + 7) // 8 * 8
     return pl.pallas_call(
         functools.partial(flow_kernel, slabs, spans),
         out_shape=jax.ShapeDtypeStruct(flow_state.shape, jnp.float32),
-        in_specs=[smem, vmem, vmem, vmem, vmem],
+        in_specs=[smem, hbm, vmem, vmem],
         out_specs=vmem,
         scratch_shapes=[
-            block, block, block,
-            pltpu.VMEM((rows_x, rows_y, rows_z), jnp.float32),
+            block, block, block, block,
+            pltpu.VMEM((turb_count + 1, rows_y, rows_z), jnp.float32),
             pltpu.VMEM((turb_count, half), jnp.float32),
-            pltpu.VMEM((rows_x, turb_count, rows_z), jnp.float32),
+            pltpu.VMEM((turb_count, half), jnp.float32),
             pltpu.VMEM((3, 2, lines, rows_z), jnp.float32),
             pltpu.VMEM((3, 2, lines, rows_z), jnp.float32),
             pltpu.VMEM((3, 2, n_comp, rows_y, rows_z), jnp.float32),
-            pltpu.SemaphoreType.DMA((3, 5)),
-            pltpu.SemaphoreType.DMA((3, 4)),
+            pltpu.VMEM((3, 8, half), jnp.float32),
+            pltpu.VMEM((3, 2, 8, half), jnp.float32),
+            pltpu.SemaphoreType.DMA((3, 7)),
+            pltpu.SemaphoreType.DMA((3, 6)),
+            pltpu.SemaphoreType.DMA,
         ],
         compiler_params=pltpu.CompilerParams(
             collective_id=0, has_side_effects=True, vmem_limit_bytes=32 << 20
         ),
         name="substeps",
-    )(plane, flow_state, blade_cells, count, weight)
+    )(table, flow_state, count, weight)
 
 
 def solution(mesh):

time: 29.2 us -> 24.5 us (0.84)
  the two profiles are of different devices: /device:TPU:4 before, /device:TPU:5 now
where the time goes in v2:
time: 24.5 us; the launch traced here: 24.3 us
  Pallas kernels  21.8 us (89%)
  local copies, waits for them, and re-layouts  2.4 us (10%)
    pallas_call x1, Pallas kernels, body(): pl.pallas_call(functools.partial(flow_kernel, slabs, spans), out_shape=ja...  17.9 us
    pallas_call x1, Pallas kernels, body(): pl.pallas_call(footprints_kernel, out_shape=(foot, foot, jax.ShapeDtypeSt...  3.93 us
    unnamed x7, local copies, waits for them, and re-layouts  2.4 us

profile of v2, /device:TPU:5, one launch (start us, length us, event | category | flops | bytes accessed | tf_op | source)
XLA Modules:
  0.0 24.3 jit_solution(8583750369935674728)
XLA Ops:
  0.0 0.0 copy-start.1
  0.0 0.9 %copy-done.1 = s32[3,64,128]{2,1,0:T(8,128)S(1)} copy-done((s32[3,64,128]{2,1,0:T(8,128)S(1)}, s32[3,64,128]{2,1,0:T(8,128)}, u32[]{:S(2)}) %copy-start.1) | copy-done | bytes 98328
  0.9 0.0 copy-start.2
  0.9 0.8 %copy-done.2 = f32[64,128]{1,0:T(8,128)S(1)} copy-done((f32[64,128]{1,0:T(8,128)S(1)}, f32[64,128]{1,0:T(8,128)}, u32[]{:S(2)}) %copy-start.2) | copy-done | bytes 32792
  1.7 0.0 copy-start
  1.7 3.9 %footprints.1 = (f32[64,16,256]{2,1,0:T(8,128)S(1)}, f32[64,16,256]{2,1,0:T(8,128)S(1)}, s32[200]{0:T(256)S(1)}) custom-call(s32[3,64,128]{2,1,0:T(8,128)S(1)} %copy-done.1, f32[64,128]{1,0:T(8,128)S(1)} %copy-done.2), custom_call_target="tpu_custom_call" | custom-call | flops 4294967296 | bytes 16777216 | tf_op jit(solution)/shard_map/footprints/pallas_call | solution.py:272
  5.6 0.0 copy-done
  5.6 17.9 %substeps.1 = f32[3,8,16,256]{3,2,1,0:T(8,128)S(1)} custom-call(s32[200]{0:T(256)S(1)} %get-tuple-element.8.table_ref, f32[3,8,16,256]{3,2,1,0:T(8,128)S(1)} %copy-done, f32[64,16,256]{2,1,0:T(8,128)S(1)} %get-tuple-element.9.count_ref, f32[64,16,256]{2,1,0:T(8,128)S(1)} %get-tuple-element.10.weight_ref), custom_call_target="tpu_custom_call" | custom-call | tf_op jit(solution)/shard_map/substeps/pallas_call | solution.py:292
  23.5 0.7 %copy.5 = f32[3,8,16,256]{3,2,1,0:T(8,128)} copy(f32[3,8,16,256]{3,2,1,0:T(8,128)S(1)} %substeps.1) | data formatting | bytes 786432
Async XLA Ops:
  0.0 0.9 %copy-start.1 = (s32[3,64,128]{2,1,0:T(8,128)S(1)}, s32[3,64,128]{2,1,0:T(8,128)}, u32[]{:S(2)}) copy-start(s32[3,64,128]{2,1,0:T(8,128)} %cells_hbm.1) | copy-start | bytes 294916
  0.9 0.8 %copy-start.2 = (f32[64,128]{1,0:T(8,128)S(1)}, f32[64,128]{1,0:T(8,128)}, u32[]{:S(2)}) copy-start(f32[64,128]{1,0:T(8,128)} %coef_hbm.1) | copy-start | bytes 98308
  1.7 3.9 %copy-start = (f32[3,8,16,256]{3,2,1,0:T(8,128)S(1)}, f32[3,8,16,256]{3,2,1,0:T(8,128)}, u32[]{:S(2)}) copy-start(f32[3,8,16,256]{3,2,1,0:T(8,128)} %start_hbm.1) | copy-start | bytes 1179652

commit v3 on v2

--- a/solution.py
+++ b/solution.py
@@ -16,14 +16,8 @@
 
 def footprints_kernel(cells_hbm, coef_hbm, count_ref, weight_ref, table_ref, cells_ref, coef_ref, heads_ref, head_ref, last_ref, link_ref, sems):
     turb_count, rows_y, rows_z = count_ref.shape
-    rows_x = last_ref.shape[0]
+    rows_x = last_ref.shape[0] - 1
     points = coef_ref.shape[1]
-
-    for i in range(3 * turb_count):
-        table_ref[i] = 0
-    for x in range(rows_x):
-        table_ref[3 * turb_count + x] = turb_count
-        last_ref[x] = -1
 
     @pl.when(lax.axis_index("sec") == 1)
     def _():
@@ -31,37 +25,55 @@
         get_coef = pltpu.make_async_copy(coef_hbm, coef_ref, sems.at[1])
         get_cells.start()
         get_coef.start()
+        for i in range(turb_count):
+            table_ref[turb_count + i] = 0
+            table_ref[2 * turb_count + i] = 0
+        for x in range(rows_x):
+            table_ref[3 * turb_count + x] = turb_count
+            last_ref[x] = -1
         count_ref[...] = jnp.zeros_like(count_ref)
-        get_cells.wait()
-        diagonal = lax.broadcasted_iota(jnp.int32, (turb_count, points), 0) == lax.broadcasted_iota(jnp.int32, (turb_count, points), 1)
-        for i in range(2):
-            heads_ref[pl.ds(i, 1), :] = jnp.sum(jnp.where(diagonal, cells_ref[i], 0), axis=0, keepdims=True)
-        to_scalars = pltpu.make_async_copy(heads_ref, head_ref, sems.at[2])
-        to_scalars.start()
         spans = lax.axis_size("gy")
         span = lax.axis_index("gy")
         first_row = span * rows_y
-        first_plane = lax.axis_index("gx") * rows_x
+        get_cells.wait()
+        diagonal = lax.broadcasted_iota(jnp.int32, (turb_count, points), 0) == lax.broadcasted_iota(jnp.int32, (turb_count, points), 1)
+        plane, start = (jnp.sum(jnp.where(diagonal, cells_ref[i], 0), axis=0, keepdims=True) for i in range(2))
+        plane = plane - lax.axis_index("gx") * rows_x
+        low = jnp.where(span == 0, spans, span) * rows_y
+        high = (span + 1) * rows_y
+        at_low = jnp.logical_or(jnp.abs(start - span * rows_y) < rows_y // 2, jnp.abs(start - low) < rows_y // 2)
+        at_high = jnp.logical_or(jnp.abs(start - high) < rows_y // 2, jnp.abs(start - jnp.where(span == spans - 1, 0, high)) < rows_y // 2)
+        near = jnp.logical_and(jnp.logical_and(plane >= 0, plane < rows_x), jnp.logical_or(at_low, at_high))
+        heads_ref[...] = jnp.broadcast_to(jnp.where(near, plane, rows_x), heads_ref.shape)
+        to_scalars = pltpu.make_async_copy(heads_ref, head_ref, sems.at[2])
+        to_scalars.start()
         to_scalars.wait()
+
+        for t in range(turb_count):
+            x = head_ref[0, t]
+            table_ref[t] = jnp.minimum(x, rows_x - 1)
+            link_ref[t] = last_ref[x]
+            last_ref[x] = t
+
+        def one_plane(x, slot):
+            def more(state):
+                return state[0] >= 0
+
+            def one(state):
+                t, k = state
+                table_ref[turb_count + k] = t
+                table_ref[2 * turb_count + k] = jnp.where(k == slot, 0, 1)
+                table_ref[3 * turb_count + x] = k
+                last_ref[rows_x] = t
+                return link_ref[t], k + 1
+
+            return lax.while_loop(more, one, (last_ref[x], slot))[1]
+
+        last_ref[rows_x] = 0
+        used = lax.fori_loop(0, rows_x, one_plane, 0)
+        for i in range(3):
+            table_ref[turb_count + jnp.minimum(used + i, turb_count - 1)] = last_ref[rows_x]
         get_coef.wait()
-
-        def chain(t, carry):
-            plane = head_ref[0, t] - first_plane
-            border = lax.div(head_ref[1, t] + rows_y // 2, rows_y)
-            above = jnp.where(border == spans, 0, border)
-            inside = jnp.logical_and(plane >= 0, plane < rows_x)
-            near = jnp.logical_and(inside, jnp.logical_or(above == span, border - 1 == span))
-            near = jnp.logical_or(near, jnp.logical_and(inside, jnp.logical_and(border == 0, span == spans - 1)))
-
-            @pl.when(near)
-            def _():
-                table_ref[t] = plane
-                link_ref[t] = last_ref[plane]
-                last_ref[plane] = t
-
-            return carry
-
-        lax.fori_loop(0, turb_count, chain, 0)
 
         def footprint(t, slot):
             y = cells_ref[1, pl.ds(t, 1), :] - first_row
@@ -75,25 +87,17 @@
                 [jnp.where(in_row, part, 0.0) for part in (jnp.full_like(coef, 1.0 / points), hi, mid, low)], axis=0
             ).astype(jnp.bfloat16)
             right = jnp.where(lax.broadcasted_iota(jnp.int32, (rows_z, points), 0) == z, 1.0, 0.0).astype(jnp.bfloat16)
-            both = lax.dot_general(left, right, (((1,), (1,)), ((), ())), preferred_element_type=jnp.float32)
-            count_ref[t] = both[:rows_y]
-            weight_ref[slot] = -(both[rows_y : 2 * rows_y] + (both[2 * rows_y : 3 * rows_y] + both[3 * rows_y :]))
-
-        def one_plane(x, slot):
-            def more(state):
-                return state[0] >= 0
-
-            def one(state):
-                t, k = state
-                footprint(t, k)
-                table_ref[turb_count + k] = t
-                table_ref[2 * turb_count + k] = jnp.where(k == slot, 0, 1)
-                table_ref[3 * turb_count + x] = k
-                return link_ref[t], k + 1
-
-            return lax.while_loop(more, one, (last_ref[x], slot))[1]
-
-        lax.fori_loop(0, rows_x, one_plane, 0)
+            return lax.dot_general(left, right, (((1,), (1,)), ((), ())), preferred_element_type=jnp.float32)
+
+        def four(i, carry):
+            slots = [4 * i + k for k in range(4)]
+            turbs = [table_ref[turb_count + slot] for slot in slots]
+            for t, slot, both in zip(turbs, slots, [footprint(t, slot) for t, slot in zip(turbs, slots)]):
+                count_ref[t] = both[:rows_y]
+                weight_ref[slot] = -(both[rows_y : 2 * rows_y] + (both[2 * rows_y : 3 * rows_y] + both[3 * rows_y :]))
+            return carry
+
+        lax.fori_loop(0, lax.div(used + 3, 4), four, 0)
 
 
 def flow_kernel(
@@ -240,7 +244,7 @@
 
         for x in range(rows_x):
             q = [now[c, x] for c in range(n_comp)]
-            drag = drag_ref[table_ref[3 * turb_count + x]]
+            drag = drag_ref[jnp.where(in_farm, table_ref[3 * turb_count + x], turb_count)]
             y_scale = viscosity + jnp.where(low_row, 0.5, -0.5) * q[1]
             for c in range(n_comp):
                 line = pl.ds(c * rows_x + x, 1)
@@ -279,7 +283,7 @@
             pltpu.VMEM(blade_coef.shape, jnp.float32),
             pltpu.VMEM((8, points), jnp.int32),
             pltpu.SMEM((8, points), jnp.int32),
-            pltpu.SMEM((rows_x,), jnp.int32),
+            pltpu.SMEM((rows_x + 1,), jnp.int32),
             pltpu.SMEM((turb_count,), jnp.int32),
             pltpu.SemaphoreType.DMA((3,)),
         ],

time: 24.5 us -> 22.5 us (0.918)
  Pallas kernels: 21.8 us -> 19.8 us
    pallas_call x1, Pallas kernels: 3.93 us -> 2.26 us  [body(): pl.pallas_call(footprints_kernel, out_shape=(foot, foot, jax.ShapeDtypeSt...]
    pallas_call x1, Pallas kernels: 17.9 us -> 17.5 us  [body(): pl.pallas_call(functools.partial(flow_kernel, slabs, spans), out_shape=ja...]
where the time goes in v3:
time: 22.5 us; the launch traced here: 22.2 us
  Pallas kernels  19.8 us (88%)
  local copies, waits for them, and re-layouts  2.4 us (11%)
    pallas_call x1, Pallas kernels, body(): pl.pallas_call(functools.partial(flow_kernel, slabs, spans), out_shape=ja...  17.5 us
    unnamed x7, local copies, waits for them, and re-layouts  2.4 us
    pallas_call x1, Pallas kernels, body(): pl.pallas_call(footprints_kernel, out_shape=(foot, foot, jax.ShapeDtypeSt...  2.26 us

profile of v3, /device:TPU:5, one launch (start us, length us, event | category | flops | bytes accessed | tf_op | source)
XLA Modules:
  0.0 22.2 jit_solution(15592939899686978087)
XLA Ops:
  0.0 0.0 copy-start.1
  0.0 0.9 %copy-done.1 = s32[3,64,128]{2,1,0:T(8,128)S(1)} copy-done((s32[3,64,128]{2,1,0:T(8,128)S(1)}, s32[3,64,128]{2,1,0:T(8,128)}, u32[]{:S(2)}) %copy-start.1) | copy-done | bytes 98328
  0.9 0.0 copy-start.2
  0.9 0.8 %copy-done.2 = f32[64,128]{1,0:T(8,128)S(1)} copy-done((f32[64,128]{1,0:T(8,128)S(1)}, f32[64,128]{1,0:T(8,128)}, u32[]{:S(2)}) %copy-start.2) | copy-done | bytes 32792
  1.7 0.0 copy-start
  1.7 2.3 %footprints.1 = (f32[64,16,256]{2,1,0:T(8,128)S(1)}, f32[64,16,256]{2,1,0:T(8,128)S(1)}, s32[200]{0:T(256)S(1)}) custom-call(s32[3,64,128]{2,1,0:T(8,128)S(1)} %copy-done.1, f32[64,128]{1,0:T(8,128)S(1)} %copy-done.2), custom_call_target="tpu_custom_call" | custom-call | flops 4294967296 | bytes 16777216 | tf_op jit(solution)/shard_map/footprints/pallas_call | solution.py:276
  3.9 0.0 copy-done
  3.9 17.5 %substeps.1 = f32[3,8,16,256]{3,2,1,0:T(8,128)S(1)} custom-call(s32[200]{0:T(256)S(1)} %get-tuple-element.8.table_ref, f32[3,8,16,256]{3,2,1,0:T(8,128)S(1)} %copy-done, f32[64,16,256]{2,1,0:T(8,128)S(1)} %get-tuple-element.9.count_ref, f32[64,16,256]{2,1,0:T(8,128)S(1)} %get-tuple-element.10.weight_ref), custom_call_target="tpu_custom_call" | custom-call | tf_op jit(solution)/shard_map/substeps/pallas_call | solution.py:296
  21.5 0.7 %copy.5 = f32[3,8,16,256]{3,2,1,0:T(8,128)} copy(f32[3,8,16,256]{3,2,1,0:T(8,128)S(1)} %substeps.1) | data formatting | bytes 786432
Async XLA Ops:
  0.0 0.9 %copy-start.1 = (s32[3,64,128]{2,1,0:T(8,128)S(1)}, s32[3,64,128]{2,1,0:T(8,128)}, u32[]{:S(2)}) copy-start(s32[3,64,128]{2,1,0:T(8,128)} %cells_hbm.1) | copy-start | bytes 294916
  0.9 0.8 %copy-start.2 = (f32[64,128]{1,0:T(8,128)S(1)}, f32[64,128]{1,0:T(8,128)}, u32[]{:S(2)}) copy-start(f32[64,128]{1,0:T(8,128)} %coef_hbm.1) | copy-start | bytes 98308
  1.7 2.3 %copy-start = (f32[3,8,16,256]{3,2,1,0:T(8,128)S(1)}, f32[3,8,16,256]{3,2,1,0:T(8,128)}, u32[]{:S(2)}) copy-start(f32[3,8,16,256]{3,2,1,0:T(8,128)} %start_hbm.1) | copy-start | bytes 1179652

commit v4 on v3

--- a/solution.py
+++ b/solution.py
@@ -142,6 +142,7 @@
     low_col, high_col = col == 0, col == rows_z - 1
     diagonal = lax.broadcasted_iota(jnp.int32, (turb_count, half), 0) == lax.broadcasted_iota(jnp.int32, (turb_count, half), 1)
 
+    pending = []
     states = (start_ref, one_ref, two_ref, out_ref)
     for stage, (keep, here, step) in enumerate(STAGES):
         now, later = states[stage], states[stage + 1]
@@ -157,8 +158,8 @@
         go_farm = remote(now.at[:, rows_x - 1], x_in.at[stage, 0], 2, 0, to_farm)
         go_above = remote(y_out.at[stage, 0], y_in.at[stage, 0], 3, 2, above)
         go_below = remote(y_out.at[stage, 1], y_in.at[stage, 1], 4, 3, below)
-        sums_above = remote(sums_out.at[stage], sums_in.at[stage, 0], 5, 4, above)
-        sums_below = remote(sums_out.at[stage], sums_in.at[stage, 1], 6, 5, below)
+        sums_above = remote(sums_out.at[stage, 0:1], sums_in.at[stage, 0, 0:1], 5, 4, above)
+        sums_below = remote(sums_out.at[stage, 0:1], sums_in.at[stage, 1, 0:1], 6, 5, below)
         for c in range(n_comp):
             for x in range(rows_x):
                 y_out[stage, 0, pl.ds(c * rows_x + x, 1), :] = now[c, x, pl.ds(rows_y - 1, 1), :]
@@ -256,6 +257,9 @@
                     rate = rate + x_in[stage, 1, c] * (viscosity - 0.5 * (q[0] + wind_speed))
                 later[c, x] = acc_ref[c, x] + step * rate
 
+        pending.append((go_right, go_left, go_farm, go_above, go_below, sums_above, sums_below))
+
+    for go_right, go_left, go_farm, go_above, go_below, sums_above, sums_below in pending:
         pl.when(has_right)(go_right.wait_send)
         pl.when(has_left)(go_left.wait_send)
         pl.when(prec_last)(go_farm.wait_send)

time: 22.5 us -> 22.2 us (0.987)
    pallas_call x1, Pallas kernels: 17.5 us -> 16.8 us  [body(): pl.pallas_call(functools.partial(flow_kernel, slabs, spans), out_shape=ja...]
    pallas_call x1, Pallas kernels: 2.26 us -> 2.78 us  [body(): pl.pallas_call(footprints_kernel, out_shape=(foot, foot, jax.ShapeDtypeSt...]
where the time goes in v4:
time: 22.2 us; the launch traced here: 22 us
  Pallas kernels  19.6 us (88%)
  local copies, waits for them, and re-layouts  2.4 us (11%)
    pallas_call x1, Pallas kernels, body(): pl.pallas_call(functools.partial(flow_kernel, slabs, spans), out_shape=ja...  16.8 us
    pallas_call x1, Pallas kernels, body(): pl.pallas_call(footprints_kernel, out_shape=(foot, foot, jax.ShapeDtypeSt...  2.78 us
    unnamed x7, local copies, waits for them, and re-layouts  2.4 us

profile of v4, /device:TPU:5, one launch (start us, length us, event | category | flops | bytes accessed | tf_op | source)
XLA Modules:
  0.0 22.0 jit_solution(17435083454079023708)
XLA Ops:
  0.0 0.0 copy-start.1
  0.0 0.9 %copy-done.1 = s32[3,64,128]{2,1,0:T(8,128)S(1)} copy-done((s32[3,64,128]{2,1,0:T(8,128)S(1)}, s32[3,64,128]{2,1,0:T(8,128)}, u32[]{:S(2)}) %copy-start.1) | copy-done | bytes 98328
  0.9 0.0 copy-start.2
  0.9 0.8 %copy-done.2 = f32[64,128]{1,0:T(8,128)S(1)} copy-done((f32[64,128]{1,0:T(8,128)S(1)}, f32[64,128]{1,0:T(8,128)}, u32[]{:S(2)}) %copy-start.2) | copy-done | bytes 32792
  1.7 0.0 copy-start
  1.7 2.8 %footprints.1 = (f32[64,16,256]{2,1,0:T(8,128)S(1)}, f32[64,16,256]{2,1,0:T(8,128)S(1)}, s32[200]{0:T(256)S(1)}) custom-call(s32[3,64,128]{2,1,0:T(8,128)S(1)} %copy-done.1, f32[64,128]{1,0:T(8,128)S(1)} %copy-done.2), custom_call_target="tpu_custom_call" | custom-call | flops 4294967296 | bytes 16777216 | tf_op jit(solution)/shard_map/footprints/pallas_call | solution.py:280
  4.4 0.0 copy-done
  4.4 16.8 %substeps.1 = f32[3,8,16,256]{3,2,1,0:T(8,128)S(1)} custom-call(s32[200]{0:T(256)S(1)} %get-tuple-element.8.table_ref, f32[3,8,16,256]{3,2,1,0:T(8,128)S(1)} %copy-done, f32[64,16,256]{2,1,0:T(8,128)S(1)} %get-tuple-element.9.count_ref, f32[64,16,256]{2,1,0:T(8,128)S(1)} %get-tuple-element.10.weight_ref), custom_call_target="tpu_custom_call" | custom-call | tf_op jit(solution)/shard_map/substeps/pallas_call | solution.py:300
  21.2 0.7 %copy.5 = f32[3,8,16,256]{3,2,1,0:T(8,128)} copy(f32[3,8,16,256]{3,2,1,0:T(8,128)S(1)} %substeps.1) | data formatting | bytes 786432
Async XLA Ops:
  0.0 0.9 %copy-start.1 = (s32[3,64,128]{2,1,0:T(8,128)S(1)}, s32[3,64,128]{2,1,0:T(8,128)}, u32[]{:S(2)}) copy-start(s32[3,64,128]{2,1,0:T(8,128)} %cells_hbm.1) | copy-start | bytes 294916
  0.9 0.8 %copy-start.2 = (f32[64,128]{1,0:T(8,128)S(1)}, f32[64,128]{1,0:T(8,128)}, u32[]{:S(2)}) copy-start(f32[64,128]{1,0:T(8,128)} %coef_hbm.1) | copy-start | bytes 98308
  1.7 2.8 %copy-start = (f32[3,8,16,256]{3,2,1,0:T(8,128)S(1)}, f32[3,8,16,256]{3,2,1,0:T(8,128)}, u32[]{:S(2)}) copy-start(f32[3,8,16,256]{3,2,1,0:T(8,128)} %start_hbm.1) | copy-start | bytes 1179652

commit v5 on v4

--- a/solution.py
+++ b/solution.py
@@ -14,17 +14,13 @@
 STAGES = ((0.0, 1.0, time_step), (0.75, 0.25, 0.25 * time_step), (1.0 / 3.0, 2.0 / 3.0, 2.0 / 3.0 * time_step))
 
 
-def footprints_kernel(cells_hbm, coef_hbm, count_ref, weight_ref, table_ref, cells_ref, coef_ref, heads_ref, head_ref, last_ref, link_ref, sems):
+def footprints_kernel(cells_ref, coef_ref, count_ref, weight_ref, table_ref, heads_ref, head_ref, last_ref, link_ref, sems):
     turb_count, rows_y, rows_z = count_ref.shape
     rows_x = last_ref.shape[0] - 1
     points = coef_ref.shape[1]
 
     @pl.when(lax.axis_index("sec") == 1)
     def _():
-        get_cells = pltpu.make_async_copy(cells_hbm, cells_ref, sems.at[0])
-        get_coef = pltpu.make_async_copy(coef_hbm, coef_ref, sems.at[1])
-        get_cells.start()
-        get_coef.start()
         for i in range(turb_count):
             table_ref[turb_count + i] = 0
             table_ref[2 * turb_count + i] = 0
@@ -35,7 +31,6 @@
         spans = lax.axis_size("gy")
         span = lax.axis_index("gy")
         first_row = span * rows_y
-        get_cells.wait()
         diagonal = lax.broadcasted_iota(jnp.int32, (turb_count, points), 0) == lax.broadcasted_iota(jnp.int32, (turb_count, points), 1)
         plane, start = (jnp.sum(jnp.where(diagonal, cells_ref[i], 0), axis=0, keepdims=True) for i in range(2))
         plane = plane - lax.axis_index("gx") * rows_x
@@ -45,7 +40,7 @@
         at_high = jnp.logical_or(jnp.abs(start - high) < rows_y // 2, jnp.abs(start - jnp.where(span == spans - 1, 0, high)) < rows_y // 2)
         near = jnp.logical_and(jnp.logical_and(plane >= 0, plane < rows_x), jnp.logical_or(at_low, at_high))
         heads_ref[...] = jnp.broadcast_to(jnp.where(near, plane, rows_x), heads_ref.shape)
-        to_scalars = pltpu.make_async_copy(heads_ref, head_ref, sems.at[2])
+        to_scalars = pltpu.make_async_copy(heads_ref, head_ref, sems.at[0])
         to_scalars.start()
         to_scalars.wait()
 
@@ -73,7 +68,6 @@
         used = lax.fori_loop(0, rows_x, one_plane, 0)
         for i in range(3):
             table_ref[turb_count + jnp.minimum(used + i, turb_count - 1)] = last_ref[rows_x]
-        get_coef.wait()
 
         def footprint(t, slot):
             y = cells_ref[1, pl.ds(t, 1), :] - first_row
@@ -280,16 +274,14 @@
     count, weight, table = pl.pallas_call(
         footprints_kernel,
         out_shape=(foot, foot, jax.ShapeDtypeStruct((3 * turb_count + rows_x,), jnp.int32)),
-        in_specs=[hbm, hbm],
+        in_specs=[vmem, vmem],
         out_specs=(vmem, vmem, smem),
         scratch_shapes=[
-            pltpu.VMEM(blade_cells.shape, jnp.int32),
-            pltpu.VMEM(blade_coef.shape, jnp.float32),
             pltpu.VMEM((8, points), jnp.int32),
             pltpu.SMEM((8, points), jnp.int32),
             pltpu.SMEM((rows_x + 1,), jnp.int32),
             pltpu.SMEM((turb_count,), jnp.int32),
-            pltpu.SemaphoreType.DMA((3,)),
+            pltpu.SemaphoreType.DMA((1,)),
         ],
         compiler_params=pltpu.CompilerParams(vmem_limit_bytes=16 << 20),
         cost_estimate=pl.CostEstimate(flops=4 << 30, bytes_accessed=16 << 20, transcendentals=0),

time: 22.2 us -> 22.3 us (level)
    pallas_call x1, Pallas kernels: 16.8 us -> 17.8 us  [body(): pl.pallas_call(functools.partial(flow_kernel, slabs, spans), out_shape=ja...]
    pallas_call x1, Pallas kernels: 2.78 us -> 1.83 us  [body(): pl.pallas_call(footprints_kernel, out_shape=(foot, foot, jax.ShapeDtypeSt...]
where the time goes in v5:
time: 22.3 us; the launch traced here: 22.1 us
  Pallas kernels  19.6 us (88%)
  local copies, waits for them, and re-layouts  2.4 us (11%)
    pallas_call x1, Pallas kernels, body(): pl.pallas_call(functools.partial(flow_kernel, slabs, spans), out_shape=ja...  17.8 us
    unnamed x7, local copies, waits for them, and re-layouts  2.4 us
    pallas_call x1, Pallas kernels, body(): pl.pallas_call(footprints_kernel, out_shape=(foot, foot, jax.ShapeDtypeSt...  1.83 us

profile of v5, /device:TPU:5, one launch (start us, length us, event | category | flops | bytes accessed | tf_op | source)
XLA Modules:
  0.0 22.1 jit_solution(7719453145439313732)
XLA Ops:
  0.0 0.0 copy-start.1
  0.0 0.9 %copy-done.1 = s32[3,64,128]{2,1,0:T(8,128)S(1)} copy-done((s32[3,64,128]{2,1,0:T(8,128)S(1)}, s32[3,64,128]{2,1,0:T(8,128)}, u32[]{:S(2)}) %copy-start.1) | copy-done | bytes 98328
  0.9 0.0 copy-start.2
  0.9 0.8 %copy-done.2 = f32[64,128]{1,0:T(8,128)S(1)} copy-done((f32[64,128]{1,0:T(8,128)S(1)}, f32[64,128]{1,0:T(8,128)}, u32[]{:S(2)}) %copy-start.2) | copy-done | bytes 32792
  1.7 0.0 copy-start
  1.7 1.8 %footprints.1 = (f32[64,16,256]{2,1,0:T(8,128)S(1)}, f32[64,16,256]{2,1,0:T(8,128)S(1)}, s32[200]{0:T(256)S(1)}) custom-call(s32[3,64,128]{2,1,0:T(8,128)S(1)} %copy-done.1, f32[64,128]{1,0:T(8,128)S(1)} %copy-done.2), custom_call_target="tpu_custom_call" | custom-call | flops 4294967296 | bytes 16777216 | tf_op jit(solution)/shard_map/footprints/pallas_call | solution.py:274
  3.5 0.0 copy-done
  3.5 17.8 %substeps.1 = f32[3,8,16,256]{3,2,1,0:T(8,128)S(1)} custom-call(s32[200]{0:T(256)S(1)} %get-tuple-element.8.table_ref, f32[3,8,16,256]{3,2,1,0:T(8,128)S(1)} %copy-done, f32[64,16,256]{2,1,0:T(8,128)S(1)} %get-tuple-element.9.count_ref, f32[64,16,256]{2,1,0:T(8,128)S(1)} %get-tuple-element.10.weight_ref), custom_call_target="tpu_custom_call" | custom-call | tf_op jit(solution)/shard_map/substeps/pallas_call | solution.py:292
  21.3 0.7 %copy.5 = f32[3,8,16,256]{3,2,1,0:T(8,128)} copy(f32[3,8,16,256]{3,2,1,0:T(8,128)S(1)} %substeps.1) | data formatting | bytes 786432
Async XLA Ops:
  0.0 0.9 %copy-start.1 = (s32[3,64,128]{2,1,0:T(8,128)S(1)}, s32[3,64,128]{2,1,0:T(8,128)}, u32[]{:S(2)}) copy-start(s32[3,64,128]{2,1,0:T(8,128)} %cells_ref.1) | copy-start | bytes 294916
  0.9 0.8 %copy-start.2 = (f32[64,128]{1,0:T(8,128)S(1)}, f32[64,128]{1,0:T(8,128)}, u32[]{:S(2)}) copy-start(f32[64,128]{1,0:T(8,128)} %coef_ref.1) | copy-start | bytes 98308
  1.7 1.8 %copy-start = (f32[3,8,16,256]{3,2,1,0:T(8,128)S(1)}, f32[3,8,16,256]{3,2,1,0:T(8,128)}, u32[]{:S(2)}) copy-start(f32[3,8,16,256]{3,2,1,0:T(8,128)} %start_hbm.1) | copy-start | bytes 1179652
